TPU v7x, 256 devices: a whole 4x4x8 slice. The times are simulated.
256 devices in a mesh: gx: 16 (over y, z_hi, core), gy: 16 (over x, z_lo).
Axes of the slice: x: 4, y: 4, z: 8 (z_hi: 2, z_lo: 4; z = z_hi * 4 + z_lo), core: 2. Of those that a mesh axis runs over, the one named last changes fastest.
Arguments:
- queries: bfloat16 [2, 4, 40, 128], replicated, may hold values from -120 to 120
- keys: bfloat16 [2, 131072, 8, 128], P(None, ('gx', 'gy')), may hold values from -6 to 6
- values: bfloat16 [2, 131072, 8, 128], P(None, ('gx', 'gy')), may hold values from -6 to 6
Outputs:
- attended: bfloat16 [2, 4, 40, 128], replicated
All inputs are finite; a program needn't handle non-finite values.
Results may differ from a plain program's by a relative error of at most 0.0011.
Values sent between devices are 32-bit elements; how exact they have to be, the bound alone decides.
No kernel may reach another device: no remote copies, remote signals or barrier semaphores. Data moves between devices by JAX's collectives and lax.ppermute only.
A program may use at most 128 MiB of HBM per device.

v0:
```python
import jax
import jax.numpy as jnp
from jax import lax
from jax.sharding import PartitionSpec as P

QH = 40
KVH = 8
HD = 128
SEQS = 2
QTOK = 4


def joined(array, axis, combine):
    everything = jax.tree.map(lambda part: lax.all_gather(part, axis), array)
    first = jax.tree.map(lambda part: part[0], everything)

    def hop(k, so_far):
        return combine(so_far, jax.tree.map(lambda part: part[k], everything))

    return lax.fori_loop(1, lax.axis_size(axis), hop, first)


def combine_parts(earlier, later):
    out_a, max_a, total_a = earlier
    out_b, max_b, total_b = later
    highest = jnp.maximum(max_a, max_b)
    factor_a = jnp.exp(max_a - highest)
    factor_b = jnp.exp(max_b - highest)
    merged_out = out_a * factor_a[..., None] + out_b * factor_b[..., None]
    return (merged_out, highest, total_a * factor_a + total_b * factor_b)


def per_device(queries, keys, values):
    scaling = HD ** (-0.5)
    group_size = QH // KVH
    grouped = queries.reshape(SEQS, QTOK, KVH, group_size, HD)
    scores = (
        jnp.einsum("sqgrd,stgd->sqgrt", grouped, keys, preferred_element_type=jnp.float32) * scaling
    )
    block_max = jnp.max(scores, axis=-1)
    weights = jnp.exp(scores - block_max[..., None])
    block_total = jnp.sum(weights, axis=-1)
    rounded_weights = weights.astype(jnp.bfloat16)
    block_out = jnp.einsum(
        "sqgrt,stgd->sqgrd", rounded_weights, values, preferred_element_type=jnp.float32
    )
    partials = (block_out, block_max, block_total)
    numerator, highest, denominator = joined(partials, ("gx", "gy"), combine_parts)
    attended = numerator / denominator[..., None]
    return attended.reshape(SEQS, QTOK, QH, HD).astype(jnp.bfloat16)


def solution(mesh):
    placed = (P(), P(None, ("gx", "gy"), None, None), P(None, ("gx", "gy"), None, None))
    return jax.shard_map(per_device, mesh=mesh, in_specs=placed, out_specs=P(), check_vma=False)
```

profile of v0, /device:TPU:32, one launch (start us, length us, event | category | flops | bytes accessed | tf_op | source)
XLA Modules:
  0.0 1907.9 jit_solution(4836877177917720364)
XLA Ops:
  6.5 1.1 copy.19
  7.6 2.5 fusion.23
  12.2 652.7 %all-gather.2 = f32[512,4,8,5]{2,1,3,0:T(4,128)S(1)} all-gather(f32[2,4,8,5]{2,1,3,0:T(4,128)S(1)} %copy.25), channel_id=4, replica_groups=mesh['gx'=16,'gy'=16] {'gx','gy'}, dimensions={0}, use_global_device_ids=true | all-gather | bytes 328960 | tf_op jit(solution)/shard_map/all_gather | solution.py:14
  664.9 2.3 copy-done.1
  667.3 654.6 %all-gather.1 = f32[512,4,8,5]{2,1,3,0:T(4,128)S(1)} all-gather(f32[2,4,8,5]{2,1,3,0:T(4,128)S(1)} %copy.24), channel_id=3, replica_groups=mesh['gx'=16,'gy'=16] {'gx','gy'}, dimensions={0}, use_global_device_ids=true | all-gather | bytes 328960 | tf_op jit(solution)/shard_map/all_gather | solution.py:14
  1321.9 2.3 copy-done.2
  1325.4 574.9 %while.19 = (s32[]{:T(128)}, f32[2,4,8,5,128]{4,3,2,1,0:T(8,128)S(1)}, f32[2,4,8,5]{3,2,1,0:T(8,128)S(1)}, f32[2,4,8,5]{3,2,1,0:T(8,128)S(1)}, f32[256,2,4,8,5]{...) while((s32[]{:T(128)}, ...), condition=%wide.region_3.0_spmd, body=%wide.region_2.0_spmd.sunk | while | flops 124805 | bytes 842383 | solution.py:20
  1326.4 0.9 constant_dynamic-slice_fusion.5
  1330.9 0.9 constant_dynamic-slice_fusion.5
  1335.4 0.9 constant_dynamic-slice_fusion.5
  1339.9 0.9 constant_dynamic-slice_fusion.5
  1344.4 0.9 constant_dynamic-slice_fusion.5
  1349.0 0.9 constant_dynamic-slice_fusion.5
  1353.5 0.9 constant_dynamic-slice_fusion.5
  1358.0 0.9 constant_dynamic-slice_fusion.5
  1360.2 0.9 constant_dynamic-slice_fusion.5
  1364.7 0.9 constant_dynamic-slice_fusion.5
  1369.2 0.9 constant_dynamic-slice_fusion.5
  1373.8 0.9 constant_dynamic-slice_fusion.5
  1378.3 0.9 constant_dynamic-slice_fusion.5
  1382.8 0.9 constant_dynamic-slice_fusion.5
  1387.3 0.9 constant_dynamic-slice_fusion.5
  1391.8 0.9 constant_dynamic-slice_fusion.5
  1396.3 0.9 constant_dynamic-slice_fusion.5
  1400.8 0.9 constant_dynamic-slice_fusion.5
  1405.3 0.9 constant_dynamic-slice_fusion.5
  1409.8 0.9 constant_dynamic-slice_fusion.5
  1414.3 0.9 constant_dynamic-slice_fusion.5
  1418.8 0.9 constant_dynamic-slice_fusion.5
  1423.4 0.9 constant_dynamic-slice_fusion.5
  1425.6 0.9 constant_dynamic-slice_fusion.5
  1430.1 0.9 constant_dynamic-slice_fusion.5
  (1526 shorter events, 548.1 us)
Async XLA Ops:
  6.5 3.6 copy-start
  6.5 1317.8 %all-gather.5.cloned.1.call-start = ((), (), s32[]{:S(2)}) async-start(), calls=%async_computation | async-start | bytes 42106880 | tf_op jit(solution)/shard_map/all_gather | solution.py:14
  664.9 2.3 copy-start.1
  1321.9 2.3 copy-start.2
Sparse Core Ops, SparseCore 0:
  11.7 779.5 all-gather.4
where the time goes:
time: 1930 us; the launch traced here: 1910 us
  blocking collectives  1310 us (68%)
  local copies, waits for them, and re-layouts  502 us (26%)
  other arithmetic  74.7 us (4%)
    all_gather x2, blocking collectives, joined(): everything = jax.tree.map(lambda part: lax.all_gather(part, axis), array)  1310 us
    dynamic_slice x1020, local copies, waits for them, and re-layouts, hop(): return combine(so_far, jax.tree.map(lambda part: part[k], everything))  493 us
    add x255, other arithmetic, combine_parts(): merged_out = out_a * factor_a[..., None] + out_b * factor_b[..., None]  64.7 us
  transfers between devices with their start and end apart: 1, of which 0 were waited for; matrix products, arithmetic and copies ran while one was open for 0% of the time, Pallas kernels for 0%

commit v1 on v0

v1 whole, which is shorter than its diff:
```python
import functools
import math

import jax
import jax.numpy as jnp
from jax import lax
from jax.experimental import pallas as pl
from jax.experimental.pallas import tpu as pltpu
from jax.sharding import PartitionSpec as P

QH = 40
KVH = 8
HD = 128
SEQS = 2
QTOK = 4
ROWS = QTOK * QH
PIECES = 16
PIECE = SEQS * ROWS // PIECES
BLOCK = 24
MAX_ROW = PIECE
TOTAL_ROW = PIECE + 1
SCALE_LOG2 = HD ** (-0.5) * math.log2(math.e)
CHUNK = 512
AXES = ("gx", "gy")
MIB = 1 << 20


def device_index(core, x, y, z):
    return ((y * 2 + z // 4) * 2 + core) * 16 + x * 4 + z % 4


SPREAD = [
    [device_index(core, x, 2 * half + (side ^ half), z) for core in range(2) for x in range(4) for side in range(2)]
    for half in range(2)
    for z in range(8)
]
HOLDERS = [
    [device_index(core, x, y, z) for y in pair for z in range(8)]
    for core in range(2)
    for x in range(4)
    for pair in ((0, 3), (1, 2))
]


def attend_kernel(q_ref, k_hbm, v_hbm, out_ref, k_buf, v_buf, scores, rows, stats, sems):
    count = k_buf.shape[1]
    copies = []
    for s in range(SEQS):
        copies.append(
            (
                pltpu.make_async_copy(k_hbm.at[s], k_buf.at[s], sems.at[2 * s]),
                pltpu.make_async_copy(v_hbm.at[s], v_buf.at[s], sems.at[2 * s + 1]),
            )
        )
    for pair in copies:
        for copy in pair:
            copy.start()
    row = lax.broadcasted_iota(jnp.int32, (ROWS, CHUNK), 0)
    lane = lax.broadcasted_iota(jnp.int32, (ROWS, CHUNK), 1)
    own_head = (row % QH) // (QH // KVH) == lane % KVH
    diagonal = row[:, :HD] % PIECE == lane[:, :HD]
    out_ref[:, PIECE:BLOCK, :] = jnp.zeros((PIECES, BLOCK - PIECE, HD), jnp.float32)
    for s in range(SEQS):
        copies[s][0].wait()
        highest = jnp.full((ROWS, HD), -1e30, jnp.float32)
        for j in range(0, count, CHUNK):
            part = lax.dot_general(
                q_ref[s],
                k_buf[s, pl.ds(j, CHUNK), :],
                (((1,), (1,)), ((), ())),
                preferred_element_type=jnp.float32,
            )
            part = jnp.where(own_head, part, -1e30)
            scores[:, pl.ds(j, CHUNK)] = part
            for i in range(0, CHUNK, HD):
                highest = jnp.maximum(highest, part[:, i : i + HD])
        block_max = jnp.max(highest, axis=1, keepdims=True)
        copies[s][1].wait()
        total = jnp.zeros((ROWS, HD), jnp.float32)
        block_out = jnp.zeros((ROWS, HD), jnp.float32)
        for j in range(0, count, CHUNK):
            weights = jnp.exp2((scores[:, pl.ds(j, CHUNK)] - block_max) * SCALE_LOG2)
            for i in range(0, CHUNK, HD):
                total = total + weights[:, i : i + HD]
            block_out = block_out + jnp.dot(
                weights.astype(jnp.bfloat16),
                v_buf[s, pl.ds(j, CHUNK), :],
                preferred_element_type=jnp.float32,
            )
        block_total = jnp.sum(total, axis=1, keepdims=True)
        rows[...] = block_out
        stats[0] = jnp.where(diagonal, block_max, 0.0)
        stats[1] = jnp.where(diagonal, block_total, 0.0)
        for p in range(ROWS // PIECE):
            at = s * (ROWS // PIECE) + p
            own = pl.ds(p * PIECE, PIECE)
            out_ref[at, 0:PIECE, :] = rows[own, :]
            out_ref[at, MAX_ROW : MAX_ROW + 1, :] = jnp.sum(stats[0, own, :], axis=0, keepdims=True)
            out_ref[at, TOTAL_ROW : TOTAL_ROW + 1, :] = jnp.sum(stats[1, own, :], axis=0, keepdims=True)


def attend(queries, keys, values):
    count = keys.shape[1]
    return pl.pallas_call(
        attend_kernel,
        out_shape=jax.ShapeDtypeStruct((PIECES, BLOCK, HD), jnp.float32),
        in_specs=[
            pl.BlockSpec(memory_space=pltpu.VMEM),
            pl.BlockSpec(memory_space=pltpu.HBM),
            pl.BlockSpec(memory_space=pltpu.HBM),
        ],
        out_specs=pl.BlockSpec(memory_space=pltpu.VMEM),
        scratch_shapes=[
            pltpu.VMEM((SEQS, count, HD), jnp.bfloat16),
            pltpu.VMEM((SEQS, count, HD), jnp.bfloat16),
            pltpu.VMEM((ROWS, count), jnp.float32),
            pltpu.VMEM((ROWS, HD), jnp.float32),
            pltpu.VMEM((2, ROWS, HD), jnp.float32),
            pltpu.SemaphoreType.DMA((2 * SEQS,)),
        ],
        compiler_params=pltpu.CompilerParams(vmem_limit_bytes=32 * MIB),
        name="attend",
    )(queries, keys, values)


def merge_kernel(last, parts_ref, out_ref):
    n = parts_ref.shape[0]
    maxima = parts_ref[:, MAX_ROW, :]
    highest = jnp.max(maxima, axis=0, keepdims=True)
    factors = jnp.exp2((maxima - highest) * SCALE_LOG2)
    total = jnp.sum(factors * parts_ref[:, TOTAL_ROW, :], axis=0, keepdims=True)
    by_row = jnp.transpose(jnp.concatenate([factors, jnp.broadcast_to(total, (8, HD))], axis=0))
    by_row = by_row[:BLOCK]
    merged = jnp.zeros((BLOCK, HD), jnp.float32)
    for i in range(n):
        merged = merged + parts_ref[i] * by_row[:, i : i + 1]
    row = lax.broadcasted_iota(jnp.int32, (BLOCK, HD), 0)
    if last:
        merged = jnp.where(row < PIECE, merged / by_row[:, n : n + 1], 0.0)
    else:
        merged = jnp.where(row < PIECE, merged, jnp.where(row == MAX_ROW, highest, total))
    for i in range(out_ref.shape[0]):
        out_ref[i] = merged


def merge(parts, copies, last):
    return pl.pallas_call(
        functools.partial(merge_kernel, last),
        out_shape=jax.ShapeDtypeStruct((copies, BLOCK, HD), jnp.float32),
        in_specs=[pl.BlockSpec(memory_space=pltpu.VMEM)],
        out_specs=pl.BlockSpec(memory_space=pltpu.VMEM),
        name="merge_last" if last else "merge",
    )(parts)


def finish_kernel(pieces_ref, out_ref):
    for s in range(SEQS):
        for q in range(QTOK):
            at = (s * QTOK + q) * (QH // PIECE)
            whole = [pieces_ref[at + i, 0:PIECE, :] for i in range(QH // PIECE)]
            out_ref[s, q] = jnp.concatenate(whole, axis=0).astype(jnp.bfloat16)


def finish(pieces):
    return pl.pallas_call(
        finish_kernel,
        out_shape=jax.ShapeDtypeStruct((SEQS, QTOK, QH, HD), jnp.bfloat16),
        in_specs=[pl.BlockSpec(memory_space=pltpu.VMEM)],
        out_specs=pl.BlockSpec(memory_space=pltpu.VMEM),
        name="finish",
    )(pieces)


def exchange(blocks, groups):
    return lax.all_to_all(blocks, AXES, 0, 0, tiled=True, axis_index_groups=groups)


def per_device(queries, keys, values):
    count = keys.shape[1] * KVH
    partials = attend(
        queries.reshape(SEQS, ROWS, HD),
        keys.reshape(SEQS, count, HD),
        values.reshape(SEQS, count, HD),
    )
    mine = merge(exchange(partials, SPREAD), len(HOLDERS[0]), False)
    done = merge(exchange(mine, HOLDERS), len(SPREAD[0]), True)
    return finish(exchange(done, SPREAD))


def solution(mesh):
    placed = (P(), P(None, AXES, None, None), P(None, AXES, None, None))
    return jax.shard_map(per_device, mesh=mesh, in_specs=placed, out_specs=P(), check_vma=False)
```

time: 1930 us -> 58.1 us (0.03)
  the two profiles are of different devices: /device:TPU:32 before, /device:TPU:1 now
where the time goes in v1:
time: 58.1 us; the launch traced here: 57.7 us
  blocking collectives  45.4 us (78%)
  Pallas kernels  8.13 us (14%)
  local copies, waits for them, and re-layouts  4.07 us (7%)
    all_to_all x3, blocking collectives, exchange(): lax.all_to_all(blocks, AXES, 0, 0, tiled=True, axis_index_groups=groups)  45.4 us
    unnamed x6, local copies, waits for them, and re-layouts  4.07 us
    pallas_call x2, Pallas kernels, merge(): pl.pallas_call(functools.partial(merge_kernel, last), out_shape=jax.Shape...  3.71 us
    pallas_call x1, Pallas kernels, attend(): pl.pallas_call(attend_kernel, out_shape=jax.ShapeDtypeStruct((PIECES, BLO...  2.85 us
    pallas_call x1, Pallas kernels, finish(): pl.pallas_call(finish_kernel, out_shape=jax.ShapeDtypeStruct((SEQS, QTOK,...  1.57 us

profile of v1, /device:TPU:1, one launch (start us, length us, event | category | flops | bytes accessed | tf_op | source)
XLA Modules:
  0.0 57.7 jit_solution(15011406480039653715)
XLA Ops:
  0.0 0.0 copy-start
  0.0 1.6 %copy-done = bf16[2,512,8,128]{3,2,1,0:T(8,128)(2,1)S(1)} copy-done((bf16[2,512,8,128]{3,2,1,0:T(8,128)(2,1)S(1)}, bf16[2,512,8,128]{3,2,1,0:T(8,128)(2,1)}, u32[]{:S(2)}) %copy-start) | copy-done | bytes 2097176
  1.6 0.0 copy-start.1
  1.6 1.6 %copy-done.1 = bf16[2,512,8,128]{3,2,1,0:T(8,128)(2,1)S(1)} copy-done((bf16[2,512,8,128]{3,2,1,0:T(8,128)(2,1)S(1)}, bf16[2,512,8,128]{3,2,1,0:T(8,128)(2,1)}, u32[]{:S(2)}) %copy-start.1) | copy-done | bytes 2097176
  3.2 0.0 copy-start.2
  3.2 0.9 %copy-done.2 = bf16[2,4,40,128]{3,2,1,0:T(8,128)(2,1)S(1)} copy-done((bf16[2,4,40,128]{3,2,1,0:T(8,128)(2,1)S(1)}, bf16[2,4,40,128]{3,2,1,0:T(8,128)(2,1)}, u32[]{:S(2)}) %copy-start.2) | copy-done | bytes 81944
  4.1 2.9 %attend.1 = f32[16,24,128]{2,1,0:T(8,128)S(1)} custom-call(bf16[2,160,128]{2,1,0:T(8,128)(2,1)S(1)} %bitcast.5, bf16[2,4096,128]{2,1,0:T(8,128)(2,1)S(1)} %bitcast.3, bf16[2,4096,128]{2,1,0:T(8,128)(2,1)S(1)} %bitcast.4), custom_call_target="tpu_custom_call" | custom-call | tf_op jit(solution)/shard_map/attend/pallas_call | solution.py:104
  6.9 13.4 %all_to_all.15.parts_ref = f32[16,24,128]{2,1,0:T(8,128)} all-to-all(f32[16,24,128]{2,1,0:T(8,128)S(1)} %attend.1), channel_id=1, replica_groups={{0,64,4,68,8,72,12,76,16,80,20,84,24,88,28,92},{1,65,5,69,9,73,13,77,17..., dimensions={0} | all-to-all | bytes 393216 | tf_op jit(solution)/shard_map/all_to_all | solution.py:175
  20.3 1.9 %merge.1 = f32[16,24,128]{2,1,0:T(8,128)} custom-call(f32[16,24,128]{2,1,0:T(8,128)} %all_to_all.15.parts_ref), custom_call_target="tpu_custom_call" | custom-call | tf_op jit(solution)/shard_map/merge/pallas_call | solution.py:147
  22.2 18.7 %all_to_all.16.parts_ref = f32[16,24,128]{2,1,0:T(8,128)} all-to-all(f32[16,24,128]{2,1,0:T(8,128)} %merge.1), channel_id=1, replica_groups={{0,1,2,3,32,33,34,35,192,193,194,195,224,225,226,227},{64,65,66,67,96,9..., dimensions={0} | all-to-all | bytes 393216 | tf_op jit(solution)/shard_map/all_to_all | solution.py:175
  40.9 1.9 %merge_last.1 = f32[16,24,128]{2,1,0:T(8,128)} custom-call(f32[16,24,128]{2,1,0:T(8,128)} %all_to_all.16.parts_ref), custom_call_target="tpu_custom_call" | custom-call | tf_op jit(solution)/shard_map/merge_last/pallas_call | solution.py:147
  42.7 13.4 %all_to_all.17.pieces_ref = f32[16,24,128]{2,1,0:T(8,128)} all-to-all(f32[16,24,128]{2,1,0:T(8,128)} %merge_last.1), channel_id=1, replica_groups={{0,64,4,68,8,72,12,76,16,80,20,84,24,88,28,92},{1,65,5,69,9,73,13,77,17..., dimensions={0} | all-to-all | bytes 393216 | tf_op jit(solution)/shard_map/all_to_all | solution.py:175
  56.1 1.6 %finish.1 = bf16[2,4,40,128]{3,2,1,0:T(8,128)(2,1)} custom-call(f32[16,24,128]{2,1,0:T(8,128)} %all_to_all.17.pieces_ref), custom_call_target="tpu_custom_call" | custom-call | tf_op jit(solution)/shard_map/finish/pallas_call | solution.py:165
Async XLA Ops:
  0.0 1.6 %copy-start = (bf16[2,512,8,128]{3,2,1,0:T(8,128)(2,1)S(1)}, bf16[2,512,8,128]{3,2,1,0:T(8,128)(2,1)}, u32[]{:S(2)}) copy-start(bf16[2,512,8,128]{3,2,1,0:T(8,128)(2,1)} %param.4) | copy-start | bytes 6291460
  1.6 1.6 %copy-start.1 = (bf16[2,512,8,128]{3,2,1,0:T(8,128)(2,1)S(1)}, bf16[2,512,8,128]{3,2,1,0:T(8,128)(2,1)}, u32[]{:S(2)}) copy-start(bf16[2,512,8,128]{3,2,1,0:T(8,128)(2,1)} %param.5) | copy-start | bytes 6291460
  3.2 0.9 %copy-start.2 = (bf16[2,4,40,128]{3,2,1,0:T(8,128)(2,1)S(1)}, bf16[2,4,40,128]{3,2,1,0:T(8,128)(2,1)}, u32[]{:S(2)}) copy-start(bf16[2,4,40,128]{3,2,1,0:T(8,128)(2,1)} %param.3) | copy-start | bytes 245764

commit v2 on v1

v2 whole, which is shorter than its diff:
```python
import functools
import math

import jax
import jax.numpy as jnp
from jax import lax
from jax.experimental import pallas as pl
from jax.experimental.pallas import tpu as pltpu
from jax.sharding import PartitionSpec as P

QH = 40
KVH = 8
HD = 128
SEQS = 2
QTOK = 4
ROWS = QTOK * QH
PIECES = 16
PIECE = SEQS * ROWS // PIECES
BLOCK = 24
MAX_ROW = PIECE
TOTAL_ROW = PIECE + 1
SCALE_LOG2 = HD ** (-0.5) * math.log2(math.e)
CHUNK = 512
LOWEST = -1e30
AXES = ("gx", "gy")
MIB = 1 << 20


def device_index(core, x, y, z):
    return ((y * 2 + z // 4) * 2 + core) * 16 + x * 4 + z % 4


SPREAD = [
    [device_index(core, 2 * half + (side ^ half), y, z) for core in range(2) for y in range(4) for side in range(2)]
    for half in range(2)
    for z in range(8)
]
HOLDERS = [
    [device_index(core, x, y, z) for x in pair for z in range(7, -1, -1)]
    for core in range(2)
    for y in range(4)
    for pair in ((0, 3), (1, 2))
]


def attend_kernel(q_hbm, k_hbm, v_hbm, out_ref, q_buf, k_buf, v_buf, scores, rows, stats, q_sem, k_sem, v_sem):
    count = k_buf.shape[1]
    q_copy = pltpu.make_async_copy(q_hbm, q_buf, q_sem)
    k_copy = [pltpu.make_async_copy(k_hbm.at[s], k_buf.at[s], k_sem.at[s]) for s in range(SEQS)]
    v_copy = [pltpu.make_async_copy(v_hbm.at[s], v_buf.at[s], v_sem.at[s]) for s in range(SEQS)]
    q_copy.start()
    for s in range(SEQS):
        k_copy[s].start()
        v_copy[s].start()
    row = lax.broadcasted_iota(jnp.int32, (ROWS, HD), 0)
    lane = lax.broadcasted_iota(jnp.int32, (ROWS, HD), 1)
    own_head = (row % QH) // (QH // KVH) == lane % KVH
    bias = jnp.where(own_head, 0.0, LOWEST).astype(jnp.float32)
    diagonal = row % PIECE == lane
    zero = jnp.zeros((ROWS, HD), jnp.float32)
    out_ref[:, PIECE:BLOCK, :] = jnp.zeros((PIECES, BLOCK - PIECE, HD), jnp.float32)

    def score(s, j, highest):
        part = lax.dot_general(
            q_buf[s],
            k_buf[s, pl.ds(j, CHUNK), :],
            (((1,), (1,)), ((), ())),
            preferred_element_type=jnp.float32,
        )
        for i in range(0, CHUNK, HD):
            own = part[:, i : i + HD] + bias
            scores[s, :, pl.ds(j + i, HD)] = own
            highest = jnp.maximum(highest, own)
        return highest

    def weigh(s, j, block_max, total, block_out):
        weights = jnp.exp2((scores[s, :, pl.ds(j, CHUNK)] - block_max) * SCALE_LOG2)
        for i in range(0, CHUNK, HD):
            total = total + weights[:, i : i + HD]
        block_out = block_out + jnp.dot(
            weights.astype(jnp.bfloat16),
            v_buf[s, pl.ds(j, CHUNK), :],
            preferred_element_type=jnp.float32,
        )
        return total, block_out

    def write(s, block_max, total, block_out):
        rows[s] = block_out
        stats[s, 0] = jnp.where(diagonal, block_max, 0.0)
        stats[s, 1] = jnp.where(diagonal, jnp.sum(total, axis=1, keepdims=True), 0.0)
        for p in range(ROWS // PIECE):
            at = s * (ROWS // PIECE) + p
            own = pl.ds(p * PIECE, PIECE)
            out_ref[at, 0:PIECE, :] = rows[s, own, :]
            out_ref[at, MAX_ROW : MAX_ROW + 1, :] = jnp.sum(stats[s, 0, own, :], axis=0, keepdims=True)
            out_ref[at, TOTAL_ROW : TOTAL_ROW + 1, :] = jnp.sum(stats[s, 1, own, :], axis=0, keepdims=True)

    q_copy.wait()
    k_copy[0].wait()
    highest = jnp.full((ROWS, HD), LOWEST, jnp.float32)
    for j in range(0, count, CHUNK):
        highest = score(0, j, highest)
    block_max = jnp.max(highest, axis=1, keepdims=True)
    for s in range(SEQS):
        if s + 1 < SEQS:
            k_copy[s + 1].wait()
        v_copy[s].wait()
        highest = jnp.full((ROWS, HD), LOWEST, jnp.float32)
        total, block_out = zero, zero
        for j in range(0, count, CHUNK):
            if s + 1 < SEQS:
                highest = score(s + 1, j, highest)
            total, block_out = weigh(s, j, block_max, total, block_out)
        write(s, block_max, total, block_out)
        block_max = jnp.max(highest, axis=1, keepdims=True)


def attend(queries, keys, values):
    count = keys.shape[1]
    return pl.pallas_call(
        attend_kernel,
        out_shape=jax.ShapeDtypeStruct((PIECES, BLOCK, HD), jnp.float32),
        in_specs=[pl.BlockSpec(memory_space=pltpu.HBM)] * 3,
        out_specs=pl.BlockSpec(memory_space=pltpu.VMEM),
        scratch_shapes=[
            pltpu.VMEM((SEQS, ROWS, HD), jnp.bfloat16),
            pltpu.VMEM((SEQS, count, HD), jnp.bfloat16),
            pltpu.VMEM((SEQS, count, HD), jnp.bfloat16),
            pltpu.VMEM((SEQS, ROWS, count), jnp.float32),
            pltpu.VMEM((SEQS, ROWS, HD), jnp.float32),
            pltpu.VMEM((SEQS, 2, ROWS, HD), jnp.float32),
            pltpu.SemaphoreType.DMA,
            pltpu.SemaphoreType.DMA((SEQS,)),
            pltpu.SemaphoreType.DMA((SEQS,)),
        ],
        compiler_params=pltpu.CompilerParams(vmem_limit_bytes=60 * MIB),
        name="attend",
    )(queries, keys, values)


def merge_kernel(last, parts_ref, out_ref):
    n = parts_ref.shape[0]
    maxima = parts_ref[:, MAX_ROW, :]
    highest = jnp.max(maxima, axis=0, keepdims=True)
    factors = jnp.exp2((maxima - highest) * SCALE_LOG2)
    total = jnp.sum(factors * parts_ref[:, TOTAL_ROW, :], axis=0, keepdims=True)
    by_row = jnp.transpose(jnp.concatenate([factors, jnp.broadcast_to(total, (8, HD))], axis=0))
    by_row = by_row[:BLOCK]
    merged = jnp.zeros((BLOCK, HD), jnp.float32)
    for i in range(n):
        merged = merged + parts_ref[i] * by_row[:, i : i + 1]
    row = lax.broadcasted_iota(jnp.int32, (BLOCK, HD), 0)
    if last:
        merged = jnp.where(row < PIECE, merged / by_row[:, n : n + 1], 0.0)
    else:
        merged = jnp.where(row < PIECE, merged, jnp.where(row == MAX_ROW, highest, total))
    for i in range(out_ref.shape[0]):
        out_ref[i] = merged


def merge(parts, copies, last):
    return pl.pallas_call(
        functools.partial(merge_kernel, last),
        out_shape=jax.ShapeDtypeStruct((copies, BLOCK, HD), jnp.float32),
        in_specs=[pl.BlockSpec(memory_space=pltpu.VMEM)],
        out_specs=pl.BlockSpec(memory_space=pltpu.VMEM),
        compiler_params=pltpu.CompilerParams(vmem_limit_bytes=4 * MIB),
        name="merge_last" if last else "merge",
    )(parts)


def finish_kernel(pieces_ref, out_ref):
    for s in range(SEQS):
        for q in range(QTOK):
            at = (s * QTOK + q) * (QH // PIECE)
            whole = [pieces_ref[at + i, 0:PIECE, :] for i in range(QH // PIECE)]
            out_ref[s, q] = jnp.concatenate(whole, axis=0).astype(jnp.bfloat16)


def finish(pieces):
    return pl.pallas_call(
        finish_kernel,
        out_shape=jax.ShapeDtypeStruct((SEQS, QTOK, QH, HD), jnp.bfloat16),
        in_specs=[pl.BlockSpec(memory_space=pltpu.VMEM)],
        out_specs=pl.BlockSpec(memory_space=pltpu.VMEM),
        compiler_params=pltpu.CompilerParams(vmem_limit_bytes=4 * MIB),
        name="finish",
    )(pieces)


def exchange(blocks, groups):
    return lax.all_to_all(blocks, AXES, 0, 0, tiled=True, axis_index_groups=groups)


def per_device(queries, keys, values):
    count = keys.shape[1] * KVH
    partials = attend(
        queries.reshape(SEQS, ROWS, HD),
        keys.reshape(SEQS, count, HD),
        values.reshape(SEQS, count, HD),
    )
    mine = merge(exchange(partials, SPREAD), len(HOLDERS[0]), False)
    done = merge(exchange(mine, HOLDERS), len(SPREAD[0]), True)
    return finish(exchange(done, SPREAD))


def solution(mesh):
    placed = (P(), P(None, AXES, None, None), P(None, AXES, None, None))
    return jax.shard_map(per_device, mesh=mesh, in_specs=placed, out_specs=P(), check_vma=False)
```

time: 58.1 us -> 48.5 us (0.83)
  local copies, waits for them, and re-layouts: 4.07 us -> 0 us
  blocking collectives: 45.4 us -> 42.7 us
  Pallas kernels: 8.13 us -> 5.5 us
    unnamed x6 -> x0, local copies, waits for them, and re-layouts: 4.07 us -> none
    pallas_call x2, Pallas kernels: 3.71 us -> 0.51 us  [merge(): pl.pallas_call(functools.partial(merge_kernel, last), out_shape=jax.Shape...]
    all_to_all x3, blocking collectives: 45.4 us -> 42.7 us  [exchange(): lax.all_to_all(blocks, AXES, 0, 0, tiled=True, axis_index_groups=groups)]
    pallas_call x1, Pallas kernels: 2.85 us -> 4.34 us  [attend(): pl.pallas_call(attend_kernel, out_shape=jax.ShapeDtypeStruct((PIECES, BLO...]
    pallas_call x1, Pallas kernels: 1.57 us -> 0.65 us  [finish(): pl.pallas_call(finish_kernel, out_shape=jax.ShapeDtypeStruct((SEQS, QTOK,...]
where the time goes in v2:
time: 48.5 us; the launch traced here: 48.2 us
  blocking collectives  42.7 us (88%)
  Pallas kernels  5.5 us (11%)
    all_to_all x3, blocking collectives, exchange(): lax.all_to_all(blocks, AXES, 0, 0, tiled=True, axis_index_groups=groups)  42.7 us
    pallas_call x1, Pallas kernels, attend(): pl.pallas_call(attend_kernel, out_shape=jax.ShapeDtypeStruct((PIECES, BLO...  4.34 us

profile of v2, /device:TPU:1, one launch (start us, length us, event | category | flops | bytes accessed | tf_op | source)
XLA Modules:
  0.0 48.2 jit_solution(5913082215307497269)
XLA Ops:
  0.0 4.3 %attend.1 = f32[16,24,128]{2,1,0:T(8,128)} custom-call(bf16[2,160,128]{2,1,0:T(8,128)(2,1)} %bitcast.5, bf16[2,4096,128]{2,1,0:T(8,128)(2,1)} %bitcast.3, bf16[2,4096,128]{2,1,0:T(8,128)(2,1)} %bitcast.4), custom_call_target="tpu_custom_call" | custom-call | tf_op jit(solution)/shard_map/attend/pallas_call | solution.py:120
  4.3 13.0 %all_to_all.15.parts_ref = f32[16,24,128]{2,1,0:T(8,128)S(1)} all-to-all(f32[16,24,128]{2,1,0:T(8,128)} %attend.1), channel_id=1, replica_groups={{0,4,64,68,128,132,192,196,16,20,80,84,144,148,208,212},{1,5,65,69,129,..., dimensions={0} | all-to-all | bytes 393216 | tf_op jit(solution)/shard_map/all_to_all | solution.py:192
  17.3 0.3 merge.1
  17.6 17.8 %all_to_all.16.parts_ref = f32[16,24,128]{2,1,0:T(8,128)S(1)} all-to-all(f32[16,24,128]{2,1,0:T(8,128)S(1)} %merge.1), channel_id=1, replica_groups={{35,34,33,32,3,2,1,0,47,46,45,44,15,14,13,12},{39,38,37,36,7,6,5,4,43,4..., dimensions={0} | all-to-all | bytes 393216 | tf_op jit(solution)/shard_map/all_to_all | solution.py:192
  35.4 0.3 merge_last.1
  35.6 11.9 %all_to_all.17.pieces_ref = f32[16,24,128]{2,1,0:T(8,128)S(1)} all-to-all(f32[16,24,128]{2,1,0:T(8,128)S(1)} %merge_last.1), channel_id=1, replica_groups={{0,4,64,68,128,132,192,196,16,20,80,84,144,148,208,212},{1,5,65,69,129,..., dimensions={0} | all-to-all | bytes 393216 | tf_op jit(solution)/shard_map/all_to_all | solution.py:192
  47.6 0.6 %finish.1 = bf16[2,4,40,128]{3,2,1,0:T(8,128)(2,1)} custom-call(f32[16,24,128]{2,1,0:T(8,128)S(1)} %all_to_all.17.pieces_ref), custom_call_target="tpu_custom_call" | custom-call | tf_op jit(solution)/shard_map/finish/pallas_call | solution.py:181

commit v3 on v2

--- a/solution.py
+++ b/solution.py
@@ -31,15 +31,15 @@
 
 
 SPREAD = [
-    [device_index(core, 2 * half + (side ^ half), y, z) for core in range(2) for y in range(4) for side in range(2)]
-    for half in range(2)
+    [device_index(core, x, y, z) for x in (2, 1, 3, 0) for y in pair for core in (1, 0)]
+    for pair in ((1, 0), (2, 3))
     for z in range(8)
 ]
 HOLDERS = [
-    [device_index(core, x, y, z) for x in pair for z in range(7, -1, -1)]
+    [device_index(core, x, y, z) for z in (4, 3, 5, 2, 6, 1, 7, 0) for y in pair]
     for core in range(2)
-    for y in range(4)
-    for pair in ((0, 3), (1, 2))
+    for x in range(4)
+    for pair in ((2, 1), (3, 0))
 ]
 
 

time: 48.5 us -> 43.9 us (0.905)
  blocking collectives: 42.7 us -> 38.1 us
    all_to_all x3, blocking collectives: 42.7 us -> 38.1 us  [exchange(): lax.all_to_all(blocks, AXES, 0, 0, tiled=True, axis_index_groups=groups)]
where the time goes in v3:
time: 43.9 us; the launch traced here: 43.7 us
  blocking collectives  38.1 us (87%)
  Pallas kernels  5.5 us (13%)
    all_to_all x3, blocking collectives, exchange(): lax.all_to_all(blocks, AXES, 0, 0, tiled=True, axis_index_groups=groups)  38.1 us
    pallas_call x1, Pallas kernels, attend(): pl.pallas_call(attend_kernel, out_shape=jax.ShapeDtypeStruct((PIECES, BLO...  4.34 us

profile of v3, /device:TPU:1, one launch (start us, length us, event | category | flops | bytes accessed | tf_op | source)
XLA Modules:
  0.0 43.7 jit_solution(7820374413500214652)
XLA Ops:
  0.0 4.3 %attend.1 = f32[16,24,128]{2,1,0:T(8,128)} custom-call(bf16[2,160,128]{2,1,0:T(8,128)(2,1)} %bitcast.5, bf16[2,4096,128]{2,1,0:T(8,128)(2,1)} %bitcast.3, bf16[2,4096,128]{2,1,0:T(8,128)(2,1)} %bitcast.4), custom_call_target="tpu_custom_call" | custom-call | tf_op jit(solution)/shard_map/attend/pallas_call | solution.py:120
  4.3 11.8 %all_to_all.15.parts_ref = f32[16,24,128]{2,1,0:T(8,128)S(1)} all-to-all(f32[16,24,128]{2,1,0:T(8,128)} %attend.1), channel_id=1, replica_groups={{88,72,24,8,84,68,20,4,92,76,28,12,80,64,16,0},{89,73,25,9,85,69,21,5,9..., dimensions={0} | all-to-all | bytes 393216 | tf_op jit(solution)/shard_map/all_to_all | solution.py:192
  16.2 0.3 merge.1
  16.4 16.1 %all_to_all.16.parts_ref = f32[16,24,128]{2,1,0:T(8,128)S(1)} all-to-all(f32[16,24,128]{2,1,0:T(8,128)S(1)} %merge.1), channel_id=1, replica_groups={{160,96,131,67,161,97,130,66,162,98,129,65,163,99,128,64},{224,32,195,3..., dimensions={0} | all-to-all | bytes 393216 | tf_op jit(solution)/shard_map/all_to_all | solution.py:192
  32.5 0.3 merge_last.1
  32.8 10.2 %all_to_all.17.pieces_ref = f32[16,24,128]{2,1,0:T(8,128)S(1)} all-to-all(f32[16,24,128]{2,1,0:T(8,128)S(1)} %merge_last.1), channel_id=1, replica_groups={{88,72,24,8,84,68,20,4,92,76,28,12,80,64,16,0},{89,73,25,9,85,69,21,5,9..., dimensions={0} | all-to-all | bytes 393216 | tf_op jit(solution)/shard_map/all_to_all | solution.py:192
  43.0 0.6 %finish.1 = bf16[2,4,40,128]{3,2,1,0:T(8,128)(2,1)} custom-call(f32[16,24,128]{2,1,0:T(8,128)S(1)} %all_to_all.17.pieces_ref), custom_call_target="tpu_custom_call" | custom-call | tf_op jit(solution)/shard_map/finish/pallas_call | solution.py:181

commit v4 on v3

--- a/solution.py
+++ b/solution.py
@@ -14,11 +14,10 @@
 SEQS = 2
 QTOK = 4
 ROWS = QTOK * QH
-PIECES = 16
+PIECES = 32
 PIECE = SEQS * ROWS // PIECES
-BLOCK = 24
-MAX_ROW = PIECE
-TOTAL_ROW = PIECE + 1
+SLABS, SLAB = 3, 4
+DONE_SLABS, DONE_SLAB = 5, 2
 SCALE_LOG2 = HD ** (-0.5) * math.log2(math.e)
 CHUNK = 512
 LOWEST = -1e30
@@ -30,17 +29,19 @@
     return ((y * 2 + z // 4) * 2 + core) * 16 + x * 4 + z % 4
 
 
-SPREAD = [
-    [device_index(core, x, y, z) for x in (2, 1, 3, 0) for y in pair for core in (1, 0)]
-    for pair in ((1, 0), (2, 3))
-    for z in range(8)
-]
+def planes(order):
+    return [[device_index(core, x, y, z) for core, x, y in order] for z in range(8)]
+
+
+SPREAD = planes([(core, x, y) for x in (2, 1, 0, 3) for y in (2, 1, 3, 0) for core in (1, 0)])
+GATHER = planes([(core, x, y) for y in (2, 1, 0, 3) for x in (2, 1, 0, 3) for core in (1, 0)])
 HOLDERS = [
-    [device_index(core, x, y, z) for z in (4, 3, 5, 2, 6, 1, 7, 0) for y in pair]
+    [device_index(core, x, y, z) for z in (4, 3, 5, 6, 0, 1, 7, 2)]
     for core in range(2)
     for x in range(4)
-    for pair in ((2, 1), (3, 0))
+    for y in range(4)
 ]
+PIECE_OF_SLOT = [SPREAD[0].index(device) for device in GATHER[0]]
 
 
 def attend_kernel(q_hbm, k_hbm, v_hbm, out_ref, q_buf, k_buf, v_buf, scores, rows, stats, q_sem, k_sem, v_sem):
@@ -58,7 +59,6 @@
     bias = jnp.where(own_head, 0.0, LOWEST).astype(jnp.float32)
     diagonal = row % PIECE == lane
     zero = jnp.zeros((ROWS, HD), jnp.float32)
-    out_ref[:, PIECE:BLOCK, :] = jnp.zeros((PIECES, BLOCK - PIECE, HD), jnp.float32)
 
     def score(s, j, highest):
         part = lax.dot_general(
@@ -90,10 +90,12 @@
         stats[s, 1] = jnp.where(diagonal, jnp.sum(total, axis=1, keepdims=True), 0.0)
         for p in range(ROWS // PIECE):
             at = s * (ROWS // PIECE) + p
+            for r in range(0, PIECE, SLAB):
+                n = min(SLAB, PIECE - r)
+                out_ref[at, r // SLAB, 0:n, :] = rows[s, pl.ds(p * PIECE + r, n), :]
             own = pl.ds(p * PIECE, PIECE)
-            out_ref[at, 0:PIECE, :] = rows[s, own, :]
-            out_ref[at, MAX_ROW : MAX_ROW + 1, :] = jnp.sum(stats[s, 0, own, :], axis=0, keepdims=True)
-            out_ref[at, TOTAL_ROW : TOTAL_ROW + 1, :] = jnp.sum(stats[s, 1, own, :], axis=0, keepdims=True)
+            for i in range(2):
+                out_ref[at, SLABS - 1, SLAB - 2 + i : SLAB - 1 + i, :] = jnp.sum(stats[s, i, own, :], axis=0, keepdims=True)
 
     q_copy.wait()
     k_copy[0].wait()
@@ -119,7 +121,7 @@
     count = keys.shape[1]
     return pl.pallas_call(
         attend_kernel,
-        out_shape=jax.ShapeDtypeStruct((PIECES, BLOCK, HD), jnp.float32),
+        out_shape=jax.ShapeDtypeStruct((PIECES, SLABS, SLAB, HD), jnp.float32),
         in_specs=[pl.BlockSpec(memory_space=pltpu.HBM)] * 3,
         out_specs=pl.BlockSpec(memory_space=pltpu.VMEM),
         scratch_shapes=[
@@ -133,35 +135,41 @@
             pltpu.SemaphoreType.DMA((SEQS,)),
             pltpu.SemaphoreType.DMA((SEQS,)),
         ],
-        compiler_params=pltpu.CompilerParams(vmem_limit_bytes=60 * MIB),
+        compiler_params=pltpu.CompilerParams(vmem_limit_bytes=32 * MIB),
         name="attend",
-    )(queries, keys, values)
+    )(*(pltpu.with_memory_space_constraint(array, pltpu.HBM) for array in (queries, keys, values)))
 
 
 def merge_kernel(last, parts_ref, out_ref):
     n = parts_ref.shape[0]
-    maxima = parts_ref[:, MAX_ROW, :]
+    maxima = parts_ref[:, SLABS - 1, SLAB - 2, :]
     highest = jnp.max(maxima, axis=0, keepdims=True)
     factors = jnp.exp2((maxima - highest) * SCALE_LOG2)
-    total = jnp.sum(factors * parts_ref[:, TOTAL_ROW, :], axis=0, keepdims=True)
+    total = jnp.sum(factors * parts_ref[:, SLABS - 1, SLAB - 1, :], axis=0, keepdims=True)
     by_row = jnp.transpose(jnp.concatenate([factors, jnp.broadcast_to(total, (8, HD))], axis=0))
-    by_row = by_row[:BLOCK]
-    merged = jnp.zeros((BLOCK, HD), jnp.float32)
-    for i in range(n):
-        merged = merged + parts_ref[i] * by_row[:, i : i + 1]
-    row = lax.broadcasted_iota(jnp.int32, (BLOCK, HD), 0)
-    if last:
-        merged = jnp.where(row < PIECE, merged / by_row[:, n : n + 1], 0.0)
-    else:
-        merged = jnp.where(row < PIECE, merged, jnp.where(row == MAX_ROW, highest, total))
-    for i in range(out_ref.shape[0]):
-        out_ref[i] = merged
+    for a in range(SLABS):
+        factor = by_row[a * SLAB : (a + 1) * SLAB]
+        merged = jnp.zeros((SLAB, HD), jnp.float32)
+        for i in range(n):
+            merged = merged + parts_ref[i, a] * factor[:, i : i + 1]
+        if last:
+            merged = merged / factor[:, n : n + 1]
+            for r in range(0, min(SLAB, PIECE - a * SLAB), DONE_SLAB):
+                done = merged[r : r + DONE_SLAB]
+                for i in range(out_ref.shape[0]):
+                    out_ref[i, (a * SLAB + r) // DONE_SLAB] = done
+        else:
+            row = lax.broadcasted_iota(jnp.int32, (SLAB, HD), 0) + a * SLAB
+            merged = jnp.where(row < PIECE, merged, jnp.where(row == PIECE, highest, total))
+            for i in range(out_ref.shape[0]):
+                out_ref[i, a] = merged
 
 
 def merge(parts, copies, last):
+    block = (DONE_SLABS, DONE_SLAB) if last else (SLABS, SLAB)
     return pl.pallas_call(
         functools.partial(merge_kernel, last),
-        out_shape=jax.ShapeDtypeStruct((copies, BLOCK, HD), jnp.float32),
+        out_shape=jax.ShapeDtypeStruct((copies, *block, HD), jnp.float32),
         in_specs=[pl.BlockSpec(memory_space=pltpu.VMEM)],
         out_specs=pl.BlockSpec(memory_space=pltpu.VMEM),
         compiler_params=pltpu.CompilerParams(vmem_limit_bytes=4 * MIB),
@@ -169,12 +177,13 @@
     )(parts)
 
 
-def finish_kernel(pieces_ref, out_ref):
+def finish_kernel(pieces_ref, out_ref, rows):
+    for slot, piece in enumerate(PIECE_OF_SLOT):
+        for a in range(DONE_SLABS):
+            rows[pl.ds(piece * PIECE + a * DONE_SLAB, DONE_SLAB), :] = pieces_ref[slot, a]
     for s in range(SEQS):
         for q in range(QTOK):
-            at = (s * QTOK + q) * (QH // PIECE)
-            whole = [pieces_ref[at + i, 0:PIECE, :] for i in range(QH // PIECE)]
-            out_ref[s, q] = jnp.concatenate(whole, axis=0).astype(jnp.bfloat16)
+            out_ref[s, q] = rows[pl.ds((s * QTOK + q) * QH, QH), :].astype(jnp.bfloat16)
 
 
 def finish(pieces):
@@ -183,6 +192,7 @@
         out_shape=jax.ShapeDtypeStruct((SEQS, QTOK, QH, HD), jnp.bfloat16),
         in_specs=[pl.BlockSpec(memory_space=pltpu.VMEM)],
         out_specs=pl.BlockSpec(memory_space=pltpu.VMEM),
+        scratch_shapes=[pltpu.VMEM((SEQS * ROWS, HD), jnp.float32)],
         compiler_params=pltpu.CompilerParams(vmem_limit_bytes=4 * MIB),
         name="finish",
     )(pieces)
@@ -200,8 +210,8 @@
         values.reshape(SEQS, count, HD),
     )
     mine = merge(exchange(partials, SPREAD), len(HOLDERS[0]), False)
-    done = merge(exchange(mine, HOLDERS), len(SPREAD[0]), True)
-    return finish(exchange(done, SPREAD))
+    done = merge(exchange(mine, HOLDERS), len(GATHER[0]), True)
+    return finish(exchange(done, GATHER))
 
 
 def solution(mesh):

time: 43.9 us -> 41.7 us (0.950)
  blocking collectives: 38.1 us -> 36.6 us
  Pallas kernels: 5.5 us -> 4.86 us
    all_to_all x3, blocking collectives: 38.1 us -> 36.6 us  [exchange(): lax.all_to_all(blocks, AXES, 0, 0, tiled=True, axis_index_groups=groups)]
    pallas_call x1, Pallas kernels: 4.34 us -> 3.71 us  [attend(): pl.pallas_call(attend_kernel, out_shape=jax.ShapeDtypeStruct((PIECES, SLA...]
where the time goes in v4:
time: 41.7 us; the launch traced here: 41.5 us
  blocking collectives  36.6 us (88%)
  Pallas kernels  4.86 us (12%)
    all_to_all x3, blocking collectives, exchange(): lax.all_to_all(blocks, AXES, 0, 0, tiled=True, axis_index_groups=groups)  36.6 us
    pallas_call x1, Pallas kernels, attend(): pl.pallas_call(attend_kernel, out_shape=jax.ShapeDtypeStruct((PIECES, SLA...  3.71 us

profile of v4, /device:TPU:1, one launch (start us, length us, event | category | flops | bytes accessed | tf_op | source)
XLA Modules:
  0.0 41.5 jit_solution(5598526627162107385)
XLA Ops:
  0.0 3.7 %attend.1 = f32[32,3,4,128]{3,2,1,0:T(4,128)S(1)} custom-call(bf16[2,160,128]{2,1,0:T(8,128)(2,1)} %bitcast.5, bf16[2,4096,128]{2,1,0:T(8,128)(2,1)} %bitcast.3, bf16[2,4096,128]{2,1,0:T(8,128)(2,1)} %bitcast.4), custom_call_target="tpu_custom_call" | custom-call | tf_op jit(solution)/shard_map/attend/pallas_call | solution.py:122
  3.7 13.2 %all_to_all.15.parts_ref = f32[32,3,4,128]{3,2,1,0:T(4,128)S(1)} all-to-all(f32[32,3,4,128]{3,2,1,0:T(4,128)S(1)} %attend.1), channel_id=1, replica_groups={{152,136,88,72,216,200,24,8,148,132,84,68,212,196,20,4,144,128,80,64,20..., dimensions={0} | all-to-all | bytes 393216 | tf_op jit(solution)/shard_map/all_to_all | solution.py:202
  16.9 0.3 merge.1
  17.2 11.7 %all_to_all.16.parts_ref = f32[8,3,4,128]{3,2,1,0:T(4,128)S(1)} all-to-all(f32[8,3,4,128]{3,2,1,0:T(4,128)S(1)} %merge.1), channel_id=1, replica_groups={{32,3,33,34,0,1,35,2},{96,67,97,98,64,65,99,66},{160,131,161,162,128,12..., dimensions={0} | all-to-all | bytes 98304 | tf_op jit(solution)/shard_map/all_to_all | solution.py:202
  28.9 0.2 merge_last.1
  29.1 11.7 %all_to_all.17.pieces_ref = f32[32,5,2,128]{3,2,1,0:T(2,128)S(1)} all-to-all(f32[32,5,2,128]{3,2,1,0:T(2,128)S(1)} %merge_last.1), channel_id=1, replica_groups={{152,136,148,132,144,128,156,140,88,72,84,68,80,64,92,76,24,8,20,4,16,0..., dimensions={0} | all-to-all | bytes 327680 | tf_op jit(solution)/shard_map/all_to_all | solution.py:202
  40.8 0.7 %finish.1 = bf16[2,4,40,128]{3,2,1,0:T(8,128)(2,1)} custom-call(f32[32,5,2,128]{3,2,1,0:T(2,128)S(1)} %all_to_all.17.pieces_ref), custom_call_target="tpu_custom_call" | custom-call | tf_op jit(solution)/shard_map/finish/pallas_call | solution.py:190

commit v5 on v4

--- a/solution.py
+++ b/solution.py
@@ -51,8 +51,8 @@
     v_copy = [pltpu.make_async_copy(v_hbm.at[s], v_buf.at[s], v_sem.at[s]) for s in range(SEQS)]
     q_copy.start()
     for s in range(SEQS):
-        k_copy[s].start()
-        v_copy[s].start()
+        k_copy[s].start(priority=0)
+        v_copy[s].start(priority=1)
     row = lax.broadcasted_iota(jnp.int32, (ROWS, HD), 0)
     lane = lax.broadcasted_iota(jnp.int32, (ROWS, HD), 1)
     own_head = (row % QH) // (QH // KVH) == lane % KVH

time: 41.7 us -> 41.4 us (level)
  no operation moved by 1% of the time
where the time goes in v5:
time: 41.4 us; the launch traced here: 41.3 us
  blocking collectives  36.6 us (88%)
  Pallas kernels  4.64 us (11%)
    all_to_all x3, blocking collectives, exchange(): lax.all_to_all(blocks, AXES, 0, 0, tiled=True, axis_index_groups=groups)  36.6 us
    pallas_call x1, Pallas kernels, attend(): pl.pallas_call(attend_kernel, out_shape=jax.ShapeDtypeStruct((PIECES, SLA...  3.49 us

profile of v5, /device:TPU:1, one launch (start us, length us, event | category | flops | bytes accessed | tf_op | source)
XLA Modules:
  0.0 41.3 jit_solution(16121620537623445428)
XLA Ops:
  0.0 3.5 %attend.1 = f32[32,3,4,128]{3,2,1,0:T(4,128)S(1)} custom-call(bf16[2,160,128]{2,1,0:T(8,128)(2,1)} %bitcast.5, bf16[2,4096,128]{2,1,0:T(8,128)(2,1)} %bitcast.3, bf16[2,4096,128]{2,1,0:T(8,128)(2,1)} %bitcast.4), custom_call_target="tpu_custom_call" | custom-call | tf_op jit(solution)/shard_map/attend/pallas_call | solution.py:122
  3.5 13.2 %all_to_all.15.parts_ref = f32[32,3,4,128]{3,2,1,0:T(4,128)S(1)} all-to-all(f32[32,3,4,128]{3,2,1,0:T(4,128)S(1)} %attend.1), channel_id=1, replica_groups={{152,136,88,72,216,200,24,8,148,132,84,68,212,196,20,4,144,128,80,64,20..., dimensions={0} | all-to-all | bytes 393216 | tf_op jit(solution)/shard_map/all_to_all | solution.py:202
  16.7 0.3 merge.1
  17.0 11.7 %all_to_all.16.parts_ref = f32[8,3,4,128]{3,2,1,0:T(4,128)S(1)} all-to-all(f32[8,3,4,128]{3,2,1,0:T(4,128)S(1)} %merge.1), channel_id=1, replica_groups={{32,3,33,34,0,1,35,2},{96,67,97,98,64,65,99,66},{160,131,161,162,128,12..., dimensions={0} | all-to-all | bytes 98304 | tf_op jit(solution)/shard_map/all_to_all | solution.py:202
  28.7 0.2 merge_last.1
  28.9 11.7 %all_to_all.17.pieces_ref = f32[32,5,2,128]{3,2,1,0:T(2,128)S(1)} all-to-all(f32[32,5,2,128]{3,2,1,0:T(2,128)S(1)} %merge_last.1), channel_id=1, replica_groups={{152,136,148,132,144,128,156,140,88,72,84,68,80,64,92,76,24,8,20,4,16,0..., dimensions={0} | all-to-all | bytes 327680 | tf_op jit(solution)/shard_map/all_to_all | solution.py:202
  40.6 0.7 %finish.1 = bf16[2,4,40,128]{3,2,1,0:T(8,128)(2,1)} custom-call(f32[32,5,2,128]{3,2,1,0:T(2,128)S(1)} %all_to_all.17.pieces_ref), custom_call_target="tpu_custom_call" | custom-call | tf_op jit(solution)/shard_map/finish/pallas_call | solution.py:190

commit v6 on v5

--- a/solution.py
+++ b/solution.py
@@ -68,13 +68,13 @@
             preferred_element_type=jnp.float32,
         )
         for i in range(0, CHUNK, HD):
-            own = part[:, i : i + HD] + bias
+            own = part[:, i : i + HD] * SCALE_LOG2 + bias
             scores[s, :, pl.ds(j + i, HD)] = own
             highest = jnp.maximum(highest, own)
         return highest
 
     def weigh(s, j, block_max, total, block_out):
-        weights = jnp.exp2((scores[s, :, pl.ds(j, CHUNK)] - block_max) * SCALE_LOG2)
+        weights = jnp.exp2(scores[s, :, pl.ds(j, CHUNK)] - block_max)
         for i in range(0, CHUNK, HD):
             total = total + weights[:, i : i + HD]
         block_out = block_out + jnp.dot(
@@ -144,7 +144,7 @@
     n = parts_ref.shape[0]
     maxima = parts_ref[:, SLABS - 1, SLAB - 2, :]
     highest = jnp.max(maxima, axis=0, keepdims=True)
-    factors = jnp.exp2((maxima - highest) * SCALE_LOG2)
+    factors = jnp.exp2(maxima - highest)
     total = jnp.sum(factors * parts_ref[:, SLABS - 1, SLAB - 1, :], axis=0, keepdims=True)
     by_row = jnp.transpose(jnp.concatenate([factors, jnp.broadcast_to(total, (8, HD))], axis=0))
     for a in range(SLABS):

time: 41.4 us -> 41.4 us (level)
  no operation moved by 1% of the time
where the time goes in v6:
time: 41.4 us; the launch traced here: 41.3 us
  blocking collectives  36.6 us (88%)
  Pallas kernels  4.62 us (11%)
    all_to_all x3, blocking collectives, exchange(): lax.all_to_all(blocks, AXES, 0, 0, tiled=True, axis_index_groups=groups)  36.6 us
    pallas_call x1, Pallas kernels, attend(): pl.pallas_call(attend_kernel, out_shape=jax.ShapeDtypeStruct((PIECES, SLA...  3.48 us

profile of v6, /device:TPU:1, one launch (start us, length us, event | category | flops | bytes accessed | tf_op | source)
XLA Modules:
  0.0 41.3 jit_solution(17721967241023067058)
XLA Ops:
  0.0 3.5 %attend.1 = f32[32,3,4,128]{3,2,1,0:T(4,128)S(1)} custom-call(bf16[2,160,128]{2,1,0:T(8,128)(2,1)} %bitcast.5, bf16[2,4096,128]{2,1,0:T(8,128)(2,1)} %bitcast.3, bf16[2,4096,128]{2,1,0:T(8,128)(2,1)} %bitcast.4), custom_call_target="tpu_custom_call" | custom-call | tf_op jit(solution)/shard_map/attend/pallas_call | solution.py:122
  3.5 13.2 %all_to_all.15.parts_ref = f32[32,3,4,128]{3,2,1,0:T(4,128)S(1)} all-to-all(f32[32,3,4,128]{3,2,1,0:T(4,128)S(1)} %attend.1), channel_id=1, replica_groups={{152,136,88,72,216,200,24,8,148,132,84,68,212,196,20,4,144,128,80,64,20..., dimensions={0} | all-to-all | bytes 393216 | tf_op jit(solution)/shard_map/all_to_all | solution.py:202
  16.7 0.3 merge.1
  17.0 11.7 %all_to_all.16.parts_ref = f32[8,3,4,128]{3,2,1,0:T(4,128)S(1)} all-to-all(f32[8,3,4,128]{3,2,1,0:T(4,128)S(1)} %merge.1), channel_id=1, replica_groups={{32,3,33,34,0,1,35,2},{96,67,97,98,64,65,99,66},{160,131,161,162,128,12..., dimensions={0} | all-to-all | bytes 98304 | tf_op jit(solution)/shard_map/all_to_all | solution.py:202
  28.7 0.2 merge_last.1
  28.9 11.7 %all_to_all.17.pieces_ref = f32[32,5,2,128]{3,2,1,0:T(2,128)S(1)} all-to-all(f32[32,5,2,128]{3,2,1,0:T(2,128)S(1)} %merge_last.1), channel_id=1, replica_groups={{152,136,148,132,144,128,156,140,88,72,84,68,80,64,92,76,24,8,20,4,16,0..., dimensions={0} | all-to-all | bytes 327680 | tf_op jit(solution)/shard_map/all_to_all | solution.py:202
  40.6 0.7 %finish.1 = bf16[2,4,40,128]{3,2,1,0:T(8,128)(2,1)} custom-call(f32[32,5,2,128]{3,2,1,0:T(2,128)S(1)} %all_to_all.17.pieces_ref), custom_call_target="tpu_custom_call" | custom-call | tf_op jit(solution)/shard_map/finish/pallas_call | solution.py:190

commit v7 on v5

--- a/solution.py
+++ b/solution.py
@@ -141,28 +141,20 @@
 
 
 def merge_kernel(last, parts_ref, out_ref):
-    n = parts_ref.shape[0]
     maxima = parts_ref[:, SLABS - 1, SLAB - 2, :]
     highest = jnp.max(maxima, axis=0, keepdims=True)
     factors = jnp.exp2((maxima - highest) * SCALE_LOG2)
     total = jnp.sum(factors * parts_ref[:, SLABS - 1, SLAB - 1, :], axis=0, keepdims=True)
-    by_row = jnp.transpose(jnp.concatenate([factors, jnp.broadcast_to(total, (8, HD))], axis=0))
-    for a in range(SLABS):
-        factor = by_row[a * SLAB : (a + 1) * SLAB]
-        merged = jnp.zeros((SLAB, HD), jnp.float32)
-        for i in range(n):
-            merged = merged + parts_ref[i, a] * factor[:, i : i + 1]
-        if last:
-            merged = merged / factor[:, n : n + 1]
-            for r in range(0, min(SLAB, PIECE - a * SLAB), DONE_SLAB):
-                done = merged[r : r + DONE_SLAB]
-                for i in range(out_ref.shape[0]):
-                    out_ref[i, (a * SLAB + r) // DONE_SLAB] = done
-        else:
-            row = lax.broadcasted_iota(jnp.int32, (SLAB, HD), 0) + a * SLAB
-            merged = jnp.where(row < PIECE, merged, jnp.where(row == PIECE, highest, total))
-            for i in range(out_ref.shape[0]):
-                out_ref[i, a] = merged
+    merged = []
+    for r in range(PIECE):
+        own = jnp.sum(parts_ref[:, r // SLAB, r % SLAB, :] * factors[:, r : r + 1], axis=0, keepdims=True)
+        merged.append(own / total[:, r : r + 1] if last else own)
+    slab = DONE_SLAB if last else SLAB
+    merged += [] if last else [highest, total]
+    for a in range(len(merged) // slab):
+        rows = jnp.concatenate(merged[a * slab : (a + 1) * slab], axis=0)
+        for i in range(out_ref.shape[0]):
+            out_ref[i, a] = rows
 
 
 def merge(parts, copies, last):

time: 41.4 us -> 41.3 us (level)
  no operation moved by 1% of the time
where the time goes in v7:
time: 41.3 us; the launch traced here: 41.1 us
  blocking collectives  36.6 us (89%)
  Pallas kernels  4.45 us (11%)
    all_to_all x3, blocking collectives, exchange(): lax.all_to_all(blocks, AXES, 0, 0, tiled=True, axis_index_groups=groups)  36.6 us
    pallas_call x1, Pallas kernels, attend(): pl.pallas_call(attend_kernel, out_shape=jax.ShapeDtypeStruct((PIECES, SLA...  3.49 us

profile of v7, /device:TPU:1, one launch (start us, length us, event | category | flops | bytes accessed | tf_op | source)
XLA Modules:
  0.0 41.1 jit_solution(2088190029331272435)
XLA Ops:
  0.0 3.5 %attend.1 = f32[32,3,4,128]{3,2,1,0:T(4,128)S(1)} custom-call(bf16[2,160,128]{2,1,0:T(8,128)(2,1)} %bitcast.5, bf16[2,4096,128]{2,1,0:T(8,128)(2,1)} %bitcast.3, bf16[2,4096,128]{2,1,0:T(8,128)(2,1)} %bitcast.4), custom_call_target="tpu_custom_call" | custom-call | tf_op jit(solution)/shard_map/attend/pallas_call | solution.py:122
  3.5 13.2 %all_to_all.15.parts_ref = f32[32,3,4,128]{3,2,1,0:T(4,128)S(1)} all-to-all(f32[32,3,4,128]{3,2,1,0:T(4,128)S(1)} %attend.1), channel_id=1, replica_groups={{152,136,88,72,216,200,24,8,148,132,84,68,212,196,20,4,144,128,80,64,20..., dimensions={0} | all-to-all | bytes 393216 | tf_op jit(solution)/shard_map/all_to_all | solution.py:194
  16.7 0.2 merge.1
  16.9 11.7 %all_to_all.16.parts_ref = f32[8,3,4,128]{3,2,1,0:T(4,128)S(1)} all-to-all(f32[8,3,4,128]{3,2,1,0:T(4,128)S(1)} %merge.1), channel_id=1, replica_groups={{32,3,33,34,0,1,35,2},{96,67,97,98,64,65,99,66},{160,131,161,162,128,12..., dimensions={0} | all-to-all | bytes 98304 | tf_op jit(solution)/shard_map/all_to_all | solution.py:194
  28.5 0.1 merge_last.1
  28.7 11.7 %all_to_all.17.pieces_ref = f32[32,5,2,128]{3,2,1,0:T(2,128)S(1)} all-to-all(f32[32,5,2,128]{3,2,1,0:T(2,128)S(1)} %merge_last.1), channel_id=1, replica_groups={{152,136,148,132,144,128,156,140,88,72,84,68,80,64,92,76,24,8,20,4,16,0..., dimensions={0} | all-to-all | bytes 327680 | tf_op jit(solution)/shard_map/all_to_all | solution.py:194
  40.4 0.7 %finish.1 = bf16[2,4,40,128]{3,2,1,0:T(8,128)(2,1)} custom-call(f32[32,5,2,128]{3,2,1,0:T(2,128)S(1)} %all_to_all.17.pieces_ref), custom_call_target="tpu_custom_call" | custom-call | tf_op jit(solution)/shard_map/finish/pallas_call | solution.py:182

commit v8 on v7

--- a/solution.py
+++ b/solution.py
@@ -68,13 +68,13 @@
             preferred_element_type=jnp.float32,
         )
         for i in range(0, CHUNK, HD):
-            own = part[:, i : i + HD] + bias
+            own = part[:, i : i + HD] * SCALE_LOG2 + bias
             scores[s, :, pl.ds(j + i, HD)] = own
             highest = jnp.maximum(highest, own)
         return highest
 
     def weigh(s, j, block_max, total, block_out):
-        weights = jnp.exp2((scores[s, :, pl.ds(j, CHUNK)] - block_max) * SCALE_LOG2)
+        weights = jnp.exp2(scores[s, :, pl.ds(j, CHUNK)] - block_max)
         for i in range(0, CHUNK, HD):
             total = total + weights[:, i : i + HD]
         block_out = block_out + jnp.dot(
@@ -143,7 +143,7 @@
 def merge_kernel(last, parts_ref, out_ref):
     maxima = parts_ref[:, SLABS - 1, SLAB - 2, :]
     highest = jnp.max(maxima, axis=0, keepdims=True)
-    factors = jnp.exp2((maxima - highest) * SCALE_LOG2)
+    factors = jnp.exp2(maxima - highest)
     total = jnp.sum(factors * parts_ref[:, SLABS - 1, SLAB - 1, :], axis=0, keepdims=True)
     merged = []
     for r in range(PIECE):

time: 41.3 us -> 41.3 us (level)
  no operation moved by 1% of the time
where the time goes in v8:
time: 41.3 us; the launch traced here: 41.1 us
  blocking collectives  36.6 us (89%)
  Pallas kernels  4.44 us (11%)
    all_to_all x3, blocking collectives, exchange(): lax.all_to_all(blocks, AXES, 0, 0, tiled=True, axis_index_groups=groups)  36.6 us
    pallas_call x1, Pallas kernels, attend(): pl.pallas_call(attend_kernel, out_shape=jax.ShapeDtypeStruct((PIECES, SLA...  3.48 us

profile of v8, /device:TPU:1, one launch (start us, length us, event | category | flops | bytes accessed | tf_op | source)
XLA Modules:
  0.0 41.1 jit_solution(18294772426616728286)
XLA Ops:
  0.0 3.5 %attend.1 = f32[32,3,4,128]{3,2,1,0:T(4,128)S(1)} custom-call(bf16[2,160,128]{2,1,0:T(8,128)(2,1)} %bitcast.5, bf16[2,4096,128]{2,1,0:T(8,128)(2,1)} %bitcast.3, bf16[2,4096,128]{2,1,0:T(8,128)(2,1)} %bitcast.4), custom_call_target="tpu_custom_call" | custom-call | tf_op jit(solution)/shard_map/attend/pallas_call | solution.py:122
  3.5 13.2 %all_to_all.15.parts_ref = f32[32,3,4,128]{3,2,1,0:T(4,128)S(1)} all-to-all(f32[32,3,4,128]{3,2,1,0:T(4,128)S(1)} %attend.1), channel_id=1, replica_groups={{152,136,88,72,216,200,24,8,148,132,84,68,212,196,20,4,144,128,80,64,20..., dimensions={0} | all-to-all | bytes 393216 | tf_op jit(solution)/shard_map/all_to_all | solution.py:194
  16.7 0.2 merge.1
  16.9 11.7 %all_to_all.16.parts_ref = f32[8,3,4,128]{3,2,1,0:T(4,128)S(1)} all-to-all(f32[8,3,4,128]{3,2,1,0:T(4,128)S(1)} %merge.1), channel_id=1, replica_groups={{32,3,33,34,0,1,35,2},{96,67,97,98,64,65,99,66},{160,131,161,162,128,12..., dimensions={0} | all-to-all | bytes 98304 | tf_op jit(solution)/shard_map/all_to_all | solution.py:194
  28.5 0.1 merge_last.1
  28.7 11.7 %all_to_all.17.pieces_ref = f32[32,5,2,128]{3,2,1,0:T(2,128)S(1)} all-to-all(f32[32,5,2,128]{3,2,1,0:T(2,128)S(1)} %merge_last.1), channel_id=1, replica_groups={{152,136,148,132,144,128,156,140,88,72,84,68,80,64,92,76,24,8,20,4,16,0..., dimensions={0} | all-to-all | bytes 327680 | tf_op jit(solution)/shard_map/all_to_all | solution.py:194
  40.4 0.7 %finish.1 = bf16[2,4,40,128]{3,2,1,0:T(8,128)(2,1)} custom-call(f32[32,5,2,128]{3,2,1,0:T(2,128)S(1)} %all_to_all.17.pieces_ref), custom_call_target="tpu_custom_call" | custom-call | tf_op jit(solution)/shard_map/finish/pallas_call | solution.py:182
